TPU v7x, 32 devices: a whole 2x2x4 slice. The times are simulated.
32 devices in a mesh: phase: 2 (over x), seq: 16 (over z, y, core).
Axes of the slice: x: 2, y: 2, z: 4, core: 2. Of those that a mesh axis runs over, the one named last changes fastest.
Arguments:
- tokens: bfloat16 [1024, 1024], P('seq'), may hold values from -6 to 6
- phase_weight: bfloat16 [2, 1024, 1024], P('phase'), may hold values from -0.1875 to 0.1875
- phase_gain: float32 [2, 1024], P('phase'), may hold values from 0.25 to 1.75
- unit_weight: bfloat16 [1024, 1024], replicated, may hold values from -0.1875 to 0.1875
- unit_gain: float32 [1024], replicated, may hold values from 0.25 to 1.75
- durations: int32 [1024], P('seq'), may hold values from 4 to 32, as said below
Outputs:
- encoder_out: bfloat16 [1024, 1024], P('seq')
- unit_states: bfloat16 [8192, 1024], P(('phase', 'seq'))
Inputs may be any that keep to these rules, and one draw needn't show every extreme that they name: durations sum to 8192; some token has exactly 32 frames and some exactly 4.
All inputs are finite; a program needn't handle non-finite values.
Results may differ from a plain program's by a relative error of at most 0.0062.
Values may be sent and summed in bfloat16 or wider, within the bound.
A program may use at most 64 MiB of HBM per device.

v0:
```python
import jax
import jax.numpy as jnp
from jax import lax
from jax.sharding import PartitionSpec as P

FR_DEV = 256


def from_behind(block, axis, distance):
    devices = range(lax.axis_size(axis))
    route = [(i - distance, i) for i in devices if i - distance in devices]
    return lax.ppermute(block, axis, route)


def from_root(array, axis, root):
    mine = lax.axis_index(axis) == root
    return lax.psum(jnp.where(mine, array, jnp.zeros_like(array)), axis)


def carried_in(array, axis, combine, identity):
    peers, mine = (lax.axis_size(axis), lax.axis_index(axis))
    everything = lax.all_gather(array, axis)
    start = jnp.broadcast_to(jnp.asarray(identity, array.dtype), array.shape)

    def turn(k, before):
        reached = k < mine
        new = combine(before, everything[k])
        return jnp.where(reached, new, before)

    return lax.fori_loop(0, peers, turn, start)


def layer(values_in, weight, gain):
    widened = values_in.astype(jnp.float32)
    scaled = widened * gain / jnp.sqrt(jnp.mean(widened * widened, axis=-1, keepdims=True) + 1e-06)
    normed = scaled.astype(jnp.bfloat16)
    branch = jax.nn.silu(jnp.dot(normed, weight, preferred_element_type=jnp.float32))
    return (widened + branch).astype(jnp.bfloat16)


def shards(tokens, phase_weight, phase_gain, unit_weight, unit_gain, durations):
    weight = phase_weight[0]
    gain_row = phase_gain[0]
    phases = lax.axis_size("phase")
    seqsize = lax.axis_size("seq")
    phase_index = lax.axis_index("phase")

    def whole_step(turn_index, current):
        return from_behind(layer(current, weight, gain_row), "phase", 1)

    hidden = layer(lax.fori_loop(0, phases - 1, whole_step, tokens), weight, gain_row)
    hidden = from_root(hidden, "phase", phases - 1)
    offset = carried_in(
        jnp.sum(durations), "seq", lambda earlier, latest: earlier + latest, jnp.int32(0)
    )
    frame_ends = offset + jnp.cumsum(durations)
    begins = frame_ends - durations
    first_frame = (phase_index * seqsize + lax.axis_index("seq")) * FR_DEV
    frames = first_frame + lax.iota(jnp.int32, FR_DEV)
    tok_count = durations.shape[0]
    min_frames = max(phases * FR_DEV // (2 * tok_count), 1)
    slot_count = min(tok_count, (FR_DEV - 2) // min_frames + 2)
    frame_low = (phase_index * seqsize + lax.iota(jnp.int32, seqsize)) * FR_DEV
    frame_high = frame_low + FR_DEV
    firsts = jnp.sum((frame_ends[None, :] <= frame_low[:, None]).astype(jnp.int32), axis=1)
    wanted = (firsts[:, None] + lax.iota(jnp.int32, slot_count)[None, :]).reshape(-1)
    clamped = jnp.minimum(wanted, tok_count - 1)
    usable = (wanted < tok_count) & (begins[clamped] < jnp.repeat(frame_high, slot_count))
    send_rows = jnp.where(usable[:, None], hidden[clamped], jnp.zeros((), jnp.bfloat16))
    send_begin = jnp.where(usable, begins[clamped], 0).astype(jnp.int32)
    send_end = jnp.where(usable, frame_ends[clamped], 0).astype(jnp.int32)
    got_rows, got_begin, got_end = (
        lax.all_to_all(send_rows, "seq", split_axis=0, concat_axis=0, tiled=True),
        lax.all_to_all(send_begin, "seq", split_axis=0, concat_axis=0, tiled=True),
        lax.all_to_all(send_end, "seq", split_axis=0, concat_axis=0, tiled=True),
    )
    member = (frames[:, None] >= got_begin[None, :]) & (frames[:, None] < got_end[None, :])
    expanded = jnp.dot(
        member.astype(jnp.bfloat16), got_rows, preferred_element_type=jnp.float32
    ).astype(jnp.bfloat16)
    unit_states = layer(expanded, unit_weight, unit_gain)
    return (hidden, unit_states)


def solution(mesh):
    return jax.shard_map(
        shards,
        mesh=mesh,
        in_specs=(P("seq", None), P("phase", None, None), P("phase", None), P(), P(), P("seq")),
        out_specs=(P("seq", None), P(("phase", "seq"), None)),
        check_vma=False,
    )
```

profile of v0, /device:TPU:13, one launch (start us, length us, event | category | flops | bytes accessed | tf_op | source)
XLA Modules:
  0.0 257.4 jit_solution(7181134546518761841)
XLA Ops:
  7.2 1.5 reduce_sum.48
  8.7 1.2 dynamic-slice
  9.9 1.4 dynamic-update-slice
  11.3 7.9 %all-reduce = s32[16]{0:T(128)S(1)} all-reduce(s32[16]{0:T(128)S(1)} %dynamic-update-slice), channel_id=1, replica_groups=mesh['phase'=2,'seq'=16] {'seq'}, use_global_device_ids=true, to_apply=%add | all-reduce | flops 16 | bytes 128
  19.2 22.2 %while.8 = (s32[]{:T(128)}, s32[]{:T(128)}, s32[]{:T(128)}, s32[16]{0:T(128)S(1)}, s32[]{:T(128)}) while((s32[]{:T(128)}, s32[]{:T(128)}, s32[]{:T(128)}, s32[16]{0:T(128)S(1)}, s32[]{:T(128)}) %tuple.221), condition=%wide.region_5.6_spmd, body=%wide.region_4.5_spmd.sunk | while | flops 5 | bytes 115 | solution.py:30
  41.4 0.7 copy.13
  44.4 0.7 fusion.52
  45.2 0.7 fusion.54
  48.9 40.1 %select_select_fusion = (s32[1024]{0:T(1024)S(1)}, pred[1024]{0:T(1024)(128)(4,1)S(1)}, pred[1024]{0:T(1024)(128)(4,1)S(1)}, pred[1024]{0:T(1024)(128)(4,1)S(1)}...) fusion(s32[]{:T(128)} %bitcast.72, s32[]{:T(128)} %bitcast.73, ...), kind=kLoop, calls=%fused_computation.53 | loop fusion | flops 129024 | bytes 72960 | tf_op jit(solution)/shard_map/gather | solution.py:71
  89.0 40.0 %select_select_fusion.1 = s32[1024]{0:T(1024)S(1)} fusion(pred[1024]{0:T(1024)(128)(4,1)S(1)} %get-tuple-element.165, pred[1024]{0:T(1024)(128)(4,1)S(1)} %get-tuple-element.164, pred[1024]{0:T(1024)(128)(4,1)S(1)} %get-tuple-element.163, pred[1024]{0:T(1024)(128)(4,1)S(1)} %get-tuple-element.162, pred[1024]{0:T(1024)(128)(4,1)S(1)} %get-tuple-element.161, ...), kind=kLoop, calls=%fused_computation.54 | loop fusion | flops 64512 | bytes 68864 | tf_op jit(solution)/shard_map/gather | solution.py:68
  129.7 8.4 %all-to-all-start.1 = ((s32[16,64,1]{1,2,0:T(1,128)}), s32[16,64,1]{1,2,0:T(1,128)S(1)}, u32[]{:S(2)}, u32[]{:S(2)}) async-start(s32[16,64,1]{1,2,0:T(1,128)} %bitcast.136), calls=%async_computation.1 | async-start | bytes 16384 | tf_op jit(solution)/shard_map/all_to_all | solution.py:75
  138.2 1.0 fusion.22
  139.3 2.3 fusion.23
  141.5 3.1 %collective-permute-start = (bf16[64,1024]{1,0:T(8,128)(2,1)S(1)}, bf16[64,1024]{1,0:T(8,128)(2,1)S(1)}, u32[]{:S(2)}, u32[]{:S(2)}) collective-permute-start(bf16[64,1024]{1,0:T(8,128)(2,1)S(1)} %fusion.23), channel_id=1, source_target_pairs={{0,16},{1,17},{2,18},{3,19},{4,20},{5,21},{6,22},{7,23},{8,24},{9,... | collective-permute-start | bytes 393224 | tf_op jit(solution)/shard_map/while/body/eval_jaxpr/ppermute | solution.py:12
  144.8 2.3 collective-permute-done
  147.3 2.8 %fusion.30 = bf16[64,1024]{1,0:T(8,128)(2,1)} fusion(bf16[1,1024,1024]{2,1,0:T(8,128)(2,1)} %param.9, bf16[64,1024]{1,0:T(8,128)(2,1)S(1)} %collective-permute-done, f32[64]{0:T(128)S(1)} %add_sqrt_fusion.1, f32[1024]{0:T(1024)S(1)} %bitcast.160, pred[]{:T(512)S(6)} %eq.3), kind=kOutput, calls=%fused_computation.37 | convolution fusion | flops 135004160 | bytes 2363649 | tf_op jit(solution)/shard_map/dot_general | solution.py:37
  150.2 23.6 %all-reduce.3.cloned.1.call-done = bf16[64,1024]{1,0:T(8,128)(2,1)} async-done(((bf16[64,1024]{1,0:T(8,128)(2,1)}), bf16[64,1024]{1,0:T(8,128)(2,1)}) %all-reduce.3.cloned.1.call-update) | async-done | bytes 131088 | tf_op jit(solution)/shard_map/psum | solution.py:17
  173.7 7.0 %gather_fusion = bf16[1024,1024]{1,0:T(8,128)(2,1)} fusion(bf16[64,1024]{1,0:T(8,128)(2,1)} %all-reduce.3.cloned.1.call-done, s32[1024]{0:T(1024)S(1)} %broadcast_clamp_fusion), kind=kCustom, calls=%fused_computation | custom fusion | bytes 4198400 | tf_op jit(solution)/shard_map/gather | solution.py:69
  180.7 6.8 %all-to-all-start = ((s32[16,64,1]{1,2,0:T(1,128)}), s32[16,64,1]{1,2,0:T(1,128)S(1)}, u32[]{:S(2)}, u32[]{:S(2)}) async-start(s32[16,64,1]{1,2,0:T(1,128)} %bitcast.71), calls=%async_computation | async-start | bytes 16384 | tf_op jit(solution)/shard_map/all_to_all | solution.py:74
  187.5 3.2 %broadcast_select_fusion = bf16[16,64,1024]{2,1,0:T(8,128)(2,1)} fusion(bf16[16,64,1024]{2,1,0:T(8,128)(2,1)} %bitcast.155, pred[16,64]{1,0:T(8,128)(4,1)S(1)} %fusion.44), kind=kLoop, calls=%fused_computation.5 | loop fusion | flops 1048576 | bytes 4195328 | tf_op jit(solution)/shard_map/jit(_where)/select_n | solution.py:69
  191.3 6.9 %all-to-all-start.2 = ((bf16[16,64,1024]{2,1,0:T(8,128)(2,1)}), bf16[16,64,1024]{2,1,0:T(8,128)(2,1)}, u32[]{:S(2)}, u32[]{:S(2)}) async-start(bf16[16,64,1024]{2,1,0:T(8,128)(2,1)} %broadcast_select_fusion), calls=%async_computation.2 | async-start | bytes 4194304 | tf_op jit(solution)/shard_map/all_to_all | solution.py:73
  200.2 45.5 %all-to-all-done.2 = bf16[16,64,1024]{2,1,0:T(8,128)(2,1)} async-done(((bf16[16,64,1024]{2,1,0:T(8,128)(2,1)}), bf16[16,64,1024]{2,1,0:T(8,128)(2,1)}, u32[]{:S(2)}, u32[]{:S(2)}) %all-to-all-start.2) | async-done | bytes 2097184 | tf_op jit(solution)/shard_map/all_to_all | solution.py:73
  245.7 2.4 fusion.6
  248.2 1.7 fusion.7
  (60 shorter events, 20.3 us)
Async XLA Ops:
  7.2 241.0 %copy-start = (bf16[1024,1024]{1,0:T(8,128)(2,1)S(1)}, bf16[1024,1024]{1,0:T(8,128)(2,1)}, u32[]{:S(2)}) copy-start(bf16[1024,1024]{1,0:T(8,128)(2,1)} %param.11) | copy-start | bytes 6291460
  89.0 58.3 %copy-start.2 = (f32[1,1024]{1,0:T(1,128)S(1)}, f32[1,1024]{1,0:T(1,128)}, u32[]{:S(2)}) copy-start(f32[1,1024]{1,0:T(1,128)} %param.10) | copy-start | bytes 12292
  129.7 51.0 %all-to-all-start.1 = ((s32[16,64,1]{1,2,0:T(1,128)}), s32[16,64,1]{1,2,0:T(1,128)S(1)}, u32[]{:S(2)}, u32[]{:S(2)}) async-start(s32[16,64,1]{1,2,0:T(1,128)} %bitcast.136), calls=%async_computation.1 | async-start | bytes 16384 | tf_op jit(solution)/shard_map/all_to_all | solution.py:75
  138.2 35.6 %all-reduce.3.cloned.1.call-start = ((), (), s32[]{:S(2)}) async-start(), calls=%async_computation.3 | async-start | bytes 262144 | tf_op jit(solution)/shard_map/psum | solution.py:17
  141.5 5.6 %collective-permute-start = (bf16[64,1024]{1,0:T(8,128)(2,1)S(1)}, bf16[64,1024]{1,0:T(8,128)(2,1)S(1)}, u32[]{:S(2)}, u32[]{:S(2)}) collective-permute-start(bf16[64,1024]{1,0:T(8,128)(2,1)S(1)} %fusion.23), channel_id=1, source_target_pairs={{0,16},{1,17},{2,18},{3,19},{4,20},{5,21},{6,22},{7,23},{8,24},{9,... | collective-permute-start | bytes 393224 | tf_op jit(solution)/shard_map/while/body/eval_jaxpr/ppermute | solution.py:12
  180.7 10.5 %all-to-all-start = ((s32[16,64,1]{1,2,0:T(1,128)}), s32[16,64,1]{1,2,0:T(1,128)S(1)}, u32[]{:S(2)}, u32[]{:S(2)}) async-start(s32[16,64,1]{1,2,0:T(1,128)} %bitcast.71), calls=%async_computation | async-start | bytes 16384 | tf_op jit(solution)/shard_map/all_to_all | solution.py:74
  191.3 54.4 %all-to-all-start.2 = ((bf16[16,64,1024]{2,1,0:T(8,128)(2,1)}), bf16[16,64,1024]{2,1,0:T(8,128)(2,1)}, u32[]{:S(2)}, u32[]{:S(2)}) async-start(bf16[16,64,1024]{2,1,0:T(8,128)(2,1)} %broadcast_select_fusion), calls=%async_computation.2 | async-start | bytes 4194304 | tf_op jit(solution)/shard_map/all_to_all | solution.py:73
  198.7 49.5 %copy-start.3 = (f32[1024]{0:T(1024)S(1)}, f32[1024]{0:T(1024)}, u32[]{:S(2)}) copy-start(f32[1024]{0:T(1024)} %param.12) | copy-start | bytes 12292
  248.2 1.7 copy-start.1
Sparse Core Ops, SparseCore 0:
  150.3 23.4 all-reduce.2
where the time goes:
time: 259 us; the launch traced here: 257 us
  other arithmetic  89.2 us (34%)
  waiting for transfers between devices  72 us (28%)
  local copies, waits for them, and re-layouts  28 us (11%)
  starting transfers between devices  25.3 us (10%)
  between operations  14.2 us (5%)
  loops' own time  11.6 us (4%)
  matrix products  9.25 us (4%)
  blocking collectives  7.88 us (3%)
    all_to_all x1, waiting for transfers between devices, shards(): lax.all_to_all(send_rows, 'seq', split_axis=0, concat_axis=0, tiled=True)  45.5 us
    gather x1, other arithmetic, shards(): send_end = jnp.where(usable, frame_ends[clamped], 0).astype(jnp.int32)  40.1 us
    gather x1, other arithmetic, shards(): begins[clamped] < jnp.repeat(frame_high, slot_count)  40 us
    psum x1, waiting for transfers between devices, from_root(): return lax.psum(jnp.where(mine, array, jnp.zeros_like(array)), axis)  23.6 us
    another operation x1, loops' own time, carried_in(): return lax.fori_loop(0, peers, turn, start)  11.6 us
    dynamic_slice x16, local copies, waits for them, and re-layouts, turn(): new = combine(before, everything[k])  10.7 us
    all_to_all x1, starting transfers between devices, shards(): lax.all_to_all(send_end, 'seq', split_axis=0, concat_axis=0, tiled=True)  8.42 us
    unnamed x1, blocking collectives  7.88 us
  transfers between devices with their start and end apart: 5, of which 4 were waited for; matrix products, arithmetic and copies ran while one was open for 7% of the time, Pallas kernels for 0%

commit v1 on v0

--- a/solution.py
+++ b/solution.py
@@ -14,7 +14,9 @@
 
 def from_root(array, axis, root):
     mine = lax.axis_index(axis) == root
-    return lax.psum(jnp.where(mine, array, jnp.zeros_like(array)), axis)
+    return jnp.sum(
+        lax.all_gather(jnp.where(mine, array, jnp.zeros_like(array)), axis_name=axis), axis=0
+    )
 
 
 def carried_in(array, axis, combine, identity):

time: 259 us -> 226 us (0.87)
  waiting for transfers between devices: 72 us -> 48.4 us
  between operations: 14.2 us -> 0.8 us
  blocking collectives: 7.88 us -> 13.1 us
    psum x1 -> x0, waiting for transfers between devices: 23.6 us -> none  [from_root(): return lax.psum(jnp.where(mine, array, jnp.zeros_like(array)), axis)]
    all_gather x0 -> x1, blocking collectives: none -> 5.22 us  [from_root(): lax.all_gather(jnp.where(mine, array, jnp.zeros_like(array)), axis_name=a...]
  transfers between devices with their start and end apart: 5 -> 4, of which waited for: 4 -> 3; matrix products, arithmetic and copies ran while one was open for 7% -> 7% of each run, Pallas kernels for 0% -> 0%
where the time goes in v1:
time: 226 us; the launch traced here: 224 us
  other arithmetic  89.2 us (39%)
  waiting for transfers between devices  48.4 us (21%)
  starting transfers between devices  26.2 us (12%)
  local copies, waits for them, and re-layouts  25.8 us (11%)
  blocking collectives  13.1 us (6%)
  loops' own time  11.6 us (5%)
  matrix products  8.59 us (4%)
    all_to_all x1, waiting for transfers between devices, shards(): lax.all_to_all(send_rows, 'seq', split_axis=0, concat_axis=0, tiled=True)  45.5 us
    gather x1, other arithmetic, shards(): send_end = jnp.where(usable, frame_ends[clamped], 0).astype(jnp.int32)  40.1 us
    gather x1, other arithmetic, shards(): begins[clamped] < jnp.repeat(frame_high, slot_count)  40 us
    another operation x1, loops' own time, carried_in(): return lax.fori_loop(0, peers, turn, start)  11.6 us
    dynamic_slice x16, local copies, waits for them, and re-layouts, turn(): new = combine(before, everything[k])  10.7 us
    all_to_all x1, starting transfers between devices, shards(): lax.all_to_all(send_end, 'seq', split_axis=0, concat_axis=0, tiled=True)  8.42 us
    unnamed x1, blocking collectives  7.88 us
    all_to_all x1, starting transfers between devices, shards(): lax.all_to_all(send_begin, 'seq', split_axis=0, concat_axis=0, tiled=True)  7.8 us
  transfers between devices with their start and end apart: 4, of which 3 were waited for; matrix products, arithmetic and copies ran while one was open for 7% of the time, Pallas kernels for 0%

profile of v1, /device:TPU:13, one launch (start us, length us, event | category | flops | bytes accessed | tf_op | source)
XLA Modules:
  0.0 223.7 jit_solution(5975949263409341543)
XLA Ops:
  0.6 1.5 reduce_sum.61
  2.2 1.2 dynamic-slice
  3.4 1.4 dynamic-update-slice
  4.8 7.9 %all-reduce = s32[16]{0:T(128)S(1)} all-reduce(s32[16]{0:T(128)S(1)} %dynamic-update-slice), channel_id=1, replica_groups=mesh['phase'=2,'seq'=16] {'seq'}, use_global_device_ids=true, to_apply=%add | all-reduce | flops 16 | bytes 128
  12.6 22.2 %while.8 = (s32[]{:T(128)}, s32[]{:T(128)}, s32[]{:T(128)}, s32[16]{0:T(128)S(1)}, s32[]{:T(128)}) while((s32[]{:T(128)}, s32[]{:T(128)}, s32[]{:T(128)}, s32[16]{0:T(128)S(1)}, s32[]{:T(128)}) %tuple.221), condition=%wide.region_5.6_spmd, body=%wide.region_4.5_spmd.sunk | while | flops 5 | bytes 115 | solution.py:32
  34.9 0.7 copy.13
  37.9 0.7 fusion.52
  38.6 0.7 fusion.54
  42.3 40.1 %select_select_fusion = (s32[1024]{0:T(1024)S(1)}, pred[1024]{0:T(1024)(128)(4,1)S(1)}, pred[1024]{0:T(1024)(128)(4,1)S(1)}, pred[1024]{0:T(1024)(128)(4,1)S(1)}...) fusion(s32[]{:T(128)} %bitcast.73, s32[]{:T(128)} %bitcast.74, ...), kind=kLoop, calls=%fused_computation.53 | loop fusion | flops 129024 | bytes 72960 | tf_op jit(solution)/shard_map/gather | solution.py:73
  82.5 40.0 %select_select_fusion.1 = s32[1024]{0:T(1024)S(1)} fusion(pred[1024]{0:T(1024)(128)(4,1)S(1)} %get-tuple-element.165, pred[1024]{0:T(1024)(128)(4,1)S(1)} %get-tuple-element.164, pred[1024]{0:T(1024)(128)(4,1)S(1)} %get-tuple-element.163, pred[1024]{0:T(1024)(128)(4,1)S(1)} %get-tuple-element.162, pred[1024]{0:T(1024)(128)(4,1)S(1)} %get-tuple-element.161, ...), kind=kLoop, calls=%fused_computation.54 | loop fusion | flops 64512 | bytes 68864 | tf_op jit(solution)/shard_map/gather | solution.py:70
  123.2 8.4 %all-to-all-start.1 = ((s32[16,64,1]{1,2,0:T(1,128)}), s32[16,64,1]{1,2,0:T(1,128)S(1)}, u32[]{:S(2)}, u32[]{:S(2)}) async-start(s32[16,64,1]{1,2,0:T(1,128)} %bitcast.137), calls=%async_computation.1 | async-start | bytes 16384 | tf_op jit(solution)/shard_map/all_to_all | solution.py:77
  131.6 1.0 fusion.22
  132.7 2.3 %fusion.23 = bf16[64,1024]{1,0:T(8,128)(2,1)S(1)} fusion(bf16[64,1024]{1,0:T(8,128)(2,1)} %param.8, bf16[1,1024,1024]{2,1,0:T(8,128)(2,1)} %param.9, f32[64]{0:T(128)S(1)} %add_sqrt_fusion.2, f32[1024]{0:T(1024)} %bitcast.161), kind=kOutput, calls=%fused_computation.32 | convolution fusion | flops 134938624 | bytes 2363648 | tf_op jit(solution)/shard_map/while/body/eval_jaxpr/dot_general | solution.py:39
  135.0 3.1 %collective-permute-start = (bf16[64,1024]{1,0:T(8,128)(2,1)S(1)}, bf16[64,1024]{1,0:T(8,128)(2,1)S(1)}, u32[]{:S(2)}, u32[]{:S(2)}) collective-permute-start(bf16[64,1024]{1,0:T(8,128)(2,1)S(1)} %fusion.23), channel_id=1, source_target_pairs={{0,16},{1,17},{2,18},{3,19},{4,20},{5,21},{6,22},{7,23},{8,24},{9,... | collective-permute-start | bytes 393224 | tf_op jit(solution)/shard_map/while/body/eval_jaxpr/ppermute | solution.py:12
  138.2 2.3 %collective-permute-done = bf16[64,1024]{1,0:T(8,128)(2,1)S(1)} collective-permute-done((bf16[64,1024]{1,0:T(8,128)(2,1)S(1)}, bf16[64,1024]{1,0:T(8,128)(2,1)S(1)}, u32[]{:S(2)}, u32[]{:S(2)}) %collective-permute-start) | collective-permute-done | bytes 131104 | tf_op jit(solution)/shard_map/while/body/eval_jaxpr/ppermute | solution.py:12
  140.7 2.2 fusion.30
  142.9 5.2 %all-gather = bf16[128,1024]{1,0:T(8,128)(2,1)S(1)} all-gather(bf16[64,1024]{1,0:T(8,128)(2,1)S(1)} %fusion.30), channel_id=2, replica_groups=mesh['phase'=2,'seq'=16] {'phase'}, dimensions={0}, use_global_device_ids=true | all-gather | bytes 393216 | tf_op jit(solution)/shard_map/all_gather | solution.py:18
  148.2 5.4 %gather_fusion = bf16[1024,1024]{1,0:T(8,128)(2,1)} fusion(bf16[64,1024]{1,0:T(8,128)(2,1)S(1)} %reduce_sum.60, s32[1024]{0:T(1024)S(1)} %broadcast_clamp_fusion), kind=kCustom, calls=%fused_computation | custom fusion | bytes 4198400 | tf_op jit(solution)/shard_map/gather | solution.py:71
  153.6 7.8 %all-to-all-start = ((s32[16,64,1]{1,2,0:T(1,128)}), s32[16,64,1]{1,2,0:T(1,128)S(1)}, u32[]{:S(2)}, u32[]{:S(2)}) async-start(s32[16,64,1]{1,2,0:T(1,128)} %bitcast.72), calls=%async_computation | async-start | bytes 16384 | tf_op jit(solution)/shard_map/all_to_all | solution.py:76
  161.4 3.2 %broadcast_select_fusion = bf16[16,64,1024]{2,1,0:T(8,128)(2,1)} fusion(bf16[16,64,1024]{2,1,0:T(8,128)(2,1)} %bitcast.156, pred[16,64]{1,0:T(8,128)(4,1)S(1)} %fusion.44), kind=kLoop, calls=%fused_computation.5 | loop fusion | flops 1048576 | bytes 4195328 | tf_op jit(solution)/shard_map/jit(_where)/select_n | solution.py:71
  165.1 6.9 %all-to-all-start.2 = ((bf16[16,64,1024]{2,1,0:T(8,128)(2,1)}), bf16[16,64,1024]{2,1,0:T(8,128)(2,1)}, u32[]{:S(2)}, u32[]{:S(2)}) async-start(bf16[16,64,1024]{2,1,0:T(8,128)(2,1)} %broadcast_select_fusion), calls=%async_computation.2 | async-start | bytes 4194304 | tf_op jit(solution)/shard_map/all_to_all | solution.py:75
  174.0 45.5 %all-to-all-done.2 = bf16[16,64,1024]{2,1,0:T(8,128)(2,1)} async-done(((bf16[16,64,1024]{2,1,0:T(8,128)(2,1)}), bf16[16,64,1024]{2,1,0:T(8,128)(2,1)}, u32[]{:S(2)}, u32[]{:S(2)}) %all-to-all-start.2) | async-done | bytes 2097184 | tf_op jit(solution)/shard_map/all_to_all | solution.py:75
  219.6 2.4 %fusion.6 = (f32[256]{0:T(256)S(1)}, bf16[256,1024]{1,0:T(8,128)(2,1)S(1)}) fusion(bf16[1024,1024]{1,0:T(8,128)(2,1)} %bitcast.139, s32[1024]{0:T(1024)S(1)} %lt.87, s32[1024]{0:T(1024)S(1)} %ge.16, s32[256]{0:T(256)S(1)} %iota_add_fusion.1), kind=kOutput, calls=%fused_computation.12 | convolution fusion | flops 538705664 | bytes 2631680 | tf_op jit(solution)/shard_map/dot_general | solution.py:80
  222.0 1.7 fusion.7
  (58 shorter events, 19.6 us)
Async XLA Ops:
  0.6 221.4 %copy-start = (bf16[1024,1024]{1,0:T(8,128)(2,1)S(1)}, bf16[1024,1024]{1,0:T(8,128)(2,1)}, u32[]{:S(2)}) copy-start(bf16[1024,1024]{1,0:T(8,128)(2,1)} %param.11) | copy-start | bytes 6291460
  82.5 58.2 %copy-start.2 = (f32[1,1024]{1,0:T(1,128)S(1)}, f32[1,1024]{1,0:T(1,128)}, u32[]{:S(2)}) copy-start(f32[1,1024]{1,0:T(1,128)} %param.10) | copy-start | bytes 12292
  123.2 30.4 %all-to-all-start.1 = ((s32[16,64,1]{1,2,0:T(1,128)}), s32[16,64,1]{1,2,0:T(1,128)S(1)}, u32[]{:S(2)}, u32[]{:S(2)}) async-start(s32[16,64,1]{1,2,0:T(1,128)} %bitcast.137), calls=%async_computation.1 | async-start | bytes 16384 | tf_op jit(solution)/shard_map/all_to_all | solution.py:77
  135.0 5.6 %collective-permute-start = (bf16[64,1024]{1,0:T(8,128)(2,1)S(1)}, bf16[64,1024]{1,0:T(8,128)(2,1)S(1)}, u32[]{:S(2)}, u32[]{:S(2)}) collective-permute-start(bf16[64,1024]{1,0:T(8,128)(2,1)S(1)} %fusion.23), channel_id=1, source_target_pairs={{0,16},{1,17},{2,18},{3,19},{4,20},{5,21},{6,22},{7,23},{8,24},{9,... | collective-permute-start | bytes 393224 | tf_op jit(solution)/shard_map/while/body/eval_jaxpr/ppermute | solution.py:12
  148.2 5.4 %copy-start.1 = (bf16[64,1024]{1,0:T(8,128)(2,1)}, bf16[64,1024]{1,0:T(8,128)(2,1)S(1)}, u32[]{:S(2)}) copy-start(bf16[64,1024]{1,0:T(8,128)(2,1)S(1)} %reduce_sum.60) | copy-start | bytes 393220
  153.6 11.5 %all-to-all-start = ((s32[16,64,1]{1,2,0:T(1,128)}), s32[16,64,1]{1,2,0:T(1,128)S(1)}, u32[]{:S(2)}, u32[]{:S(2)}) async-start(s32[16,64,1]{1,2,0:T(1,128)} %bitcast.72), calls=%async_computation | async-start | bytes 16384 | tf_op jit(solution)/shard_map/all_to_all | solution.py:76
  165.1 54.4 %all-to-all-start.2 = ((bf16[16,64,1024]{2,1,0:T(8,128)(2,1)}), bf16[16,64,1024]{2,1,0:T(8,128)(2,1)}, u32[]{:S(2)}, u32[]{:S(2)}) async-start(bf16[16,64,1024]{2,1,0:T(8,128)(2,1)} %broadcast_select_fusion), calls=%async_computation.2 | async-start | bytes 4194304 | tf_op jit(solution)/shard_map/all_to_all | solution.py:75
  172.5 49.5 %copy-start.3 = (f32[1024]{0:T(1024)S(1)}, f32[1024]{0:T(1024)}, u32[]{:S(2)}) copy-start(f32[1024]{0:T(1024)} %param.12) | copy-start | bytes 12292
